TPU v7x, 32 devices: a whole 2x2x4 slice. The times are simulated.
32 devices in a mesh: row: 8 (over z, x), col: 4 (over y, core).
Axes of the slice: x: 2, y: 2, z: 4, core: 2. Of those that a mesh axis runs over, the one named last changes fastest.
Arguments:
- activations: bfloat16 [512, 12288], P('col', 'row'), may hold values from -6 to 6
- weight_tiles: bfloat16 [4, 8, 12, 4096], P('col', 'row'), may hold values from -0.125 to 0.125
- tile_ids: int32 [4, 8, 12], P('col', 'row'), may hold values from 0 to 2303, as said below
- tile_counts: int32 [4, 8], P('col', 'row'), may hold values from 7 to 12, as said below
- upstream: bfloat16 [512, 24576], P('col', 'row'), may hold values from -0.119628906 to 0.119628906
Outputs:
- output: bfloat16 [512, 24576], P('col', 'row')
- weight_grad: bfloat16 [4, 8, 12, 4096], P('col', 'row')
Inputs may be any that keep to these rules, and one draw needn't show every extreme that they name: `tile_ids`: within one block the 12 slots name distinct tiles; only slots below the block's count are used. `tile_counts`: some block is full in every draw.
All inputs are finite; a program needn't handle non-finite values.
Results may differ from a plain program's by a relative error of at most 0.017.
Values may be sent and summed in bfloat16 or wider, within the bound.
A program may use at most 64 MiB of HBM per device.

v0:
```python
import jax
import jax.numpy as jnp
from jax import lax
from jax.sharding import PartitionSpec as P

TILE = 64
CAP = 12


def gelu_parts(pre):
    cumul = 0.5 * (1.0 + jax.scipy.special.erf(pre * 0.7071067811865476))
    density = jnp.exp(-0.5 * pre * pre) * 0.3989422804014327
    return (cumul, density)


def body(activations, weight_tiles, tile_ids, tile_counts, upstream):
    panels, slot_ids, slot_counts = (
        lax.all_gather(weight_tiles, "col", axis=0, tiled=True),
        lax.all_gather(tile_ids, "col", axis=0, tiled=True),
        lax.all_gather(tile_counts, "col", axis=0, tiled=True),
    )
    features = lax.all_gather(activations, "row", axis=1, tiled=True)
    columns = lax.axis_size("col")
    tok_rows = activations.shape[0]
    width = features.shape[1]
    ff_local = upstream.shape[1]
    per_col = ff_local // TILE
    d_block = width // columns // TILE
    slots = columns * CAP
    tiles = panels.reshape(slots, TILE, TILE)
    slot_flat = slot_ids.reshape(slots)
    owner = jnp.arange(slots, dtype=jnp.int32) // CAP
    position = jnp.arange(slots, dtype=jnp.int32) % CAP
    live = position < slot_counts.reshape(columns)[owner]
    d_tile = owner * d_block + slot_flat // per_col
    f_tile = slot_flat % per_col
    placing = (
        (f_tile[:, None] == jnp.arange(per_col, dtype=jnp.int32)[None, :]) & live[:, None]
    ).astype(jnp.float32)
    x_tiles = jnp.take(features.reshape(tok_rows, width // TILE, TILE), d_tile, axis=1)
    partial_value = jnp.einsum("tsk,skn->tsn", x_tiles, tiles, preferred_element_type=jnp.float32)
    pre = jnp.einsum(
        "tsn,sf->tfn", partial_value, placing, precision=lax.Precision.HIGHEST
    ).reshape(tok_rows, ff_local)
    cumul, density = gelu_parts(pre)
    output = (pre * cumul).astype(jnp.bfloat16)
    grad_pre = (upstream.astype(jnp.float32) * (cumul + pre * density)).astype(jnp.bfloat16)
    g_tiles = jnp.take(grad_pre.reshape(tok_rows, per_col, TILE), f_tile, axis=1)
    own_live = jnp.arange(CAP, dtype=jnp.int32) < tile_counts.reshape(())
    term = jnp.einsum("tsk,tsn->skn", x_tiles, g_tiles, preferred_element_type=jnp.float32).reshape(
        slots, TILE * TILE
    )
    summed = lax.psum_scatter(
        term.astype(jnp.bfloat16), "col", scatter_dimension=0, tiled=True
    ).astype(jnp.float32)
    grad = jnp.where(own_live[:, None], summed, 0.0).astype(jnp.bfloat16)
    return (output, grad.reshape(1, 1, CAP, TILE * TILE))


def solution(mesh):
    return jax.shard_map(
        body,
        mesh=mesh,
        in_specs=(
            P("col", "row"),
            P("col", "row", None, None),
            P("col", "row", None),
            P("col", "row"),
            P("col", "row"),
        ),
        out_specs=(P("col", "row"), P("col", "row", None, None)),
        check_vma=False,
    )
```

profile of v0, /device:TPU:1, one launch (start us, length us, event | category | flops | bytes accessed | tf_op | source)
XLA Modules:
  0.0 105.0 jit_solution(8885097372242348135)
XLA Ops:
  7.2 0.0 copy-start
  7.2 0.0 all-gather.2.cloned.1.call-start
  7.2 2.0 %copy.16 = bf16[128,1536]{0,1:T(8,128)(2,1)} copy(bf16[128,1536]{1,0:T(8,128)(2,1)} %param.5) | data formatting | bytes 786432 | tf_op args[0]
  9.2 0.0 all-gather.2.cloned.1.call-update
  9.9 1.3 %fusion.38 = (u32[1]{0:T(128)}, u32[1]{0:T(128)}) fusion(u32[32]{0:T(128)} %constant.85, u32[]{:S(6)} %partition-id.5, u32[]{:T(128)S(6)} %add.144), kind=kLoop, calls=%fused_computation.73 | loop fusion | bytes 24
  11.2 0.7 bitcast_dynamic-update-slice_fusion
  11.9 5.1 %all-reduce = s32[4]{0:T(128)S(1)} all-reduce(s32[4]{0:T(128)S(1)} %bitcast_dynamic-update-slice_fusion), channel_id=1, replica_groups=mesh['row'=8,'col'=4] {'col'}, use_global_device_ids=true, to_apply=%add | all-reduce | flops 4 | bytes 32
  17.0 6.3 %all_gather.12 = s32[4,1,12]{2,1,0:T(1,128)S(1)} all-gather(s32[1,1,12]{2,1,0:T(1,128)} %param.7), channel_id=1, replica_groups=mesh['row'=8,'col'=4] {'col'}, dimensions={0}, use_global_device_ids=true | all-gather | bytes 240 | tf_op jit(solution)/shard_map/all_gather | solution.py:19
  23.3 0.1 ne.134
  23.4 0.1 ne.135
  23.5 0.5 broadcast.336
  24.0 0.7 fusion.37
  24.7 0.1 div.45
  24.8 0.1 rem.74
  24.9 0.1 div.46
  25.0 0.1 rem.81
  25.0 7.5 %all_gather.15 = bf16[4,1,12,4096]{3,2,1,0:T(8,128)(2,1)S(1)} all-gather(bf16[1,1,12,4096]{3,2,1,0:T(8,128)(2,1)} %param.6), channel_id=1, replica_groups=mesh['row'=8,'col'=4] {'col'}, dimensions={0}, use_global_device_ids=true | all-gather | bytes 491520 | tf_op jit(solution)/shard_map/all_gather | solution.py:18
  32.5 0.8 reshape.200
  33.4 0.0 copy-done
  33.4 0.4 copy.20
  34.4 0.7 fusion.39
  35.0 2.5 %fusion.28 = pred[48]{0:T(512)(128)(4,1)S(1)} fusion(s32[]{:T(128)} %bitcast.2, s32[]{:T(128)} %bitcast.3, s32[]{:T(128)} %bitcast.5, s32[]{:T(128)} %bitcast.4), kind=kLoop, calls=%fused_computation.60 | loop fusion | flops 1152 | bytes 64 | tf_op jit(solution)/shard_map/lt | solution.py:34
  37.7 34.8 %all-gather.2.cloned.1.call-done = bf16[128,12288]{0,1:T(8,128)(2,1)} async-done(((bf16[128,1536]{0,1:T(8,128)(2,1)}), bf16[128,12288]{0,1:T(8,128)(2,1)}) %all-gather.2.cloned.1.call-update) | async-done | bytes 3145744 | tf_op jit(solution)/shard_map/all_gather | solution.py:22
  72.5 2.6 %gather_fusion = bf16[48,128,64]{1,2,0:T(8,128)(2,1)S(1)} fusion(bf16[128,192,64]{0,2,1:T(8,128)(2,1)} %bitcast.59, s32[1024]{0:T(1024)S(1)} %pad_clamp_fusion.1), kind=kCustom, calls=%fused_computation | custom fusion | bytes 1573056 | tf_op jit(solution)/shard_map/jit(_take)/gather | solution.py:40
  75.1 0.5 convolution_bitcast_fusion
  75.6 1.9 %fusion.13 = f32[128,48,64]{0,1,2:T(8,128)S(1)} fusion(f32[128,48,64]{0,2,1:T(8,128)S(1)} %convolution_bitcast_fusion, s32[48]{0:T(128)S(1)} %get-tuple-element.9, pred[48]{0:T(512)(128)(4,1)S(1)} %fusion.28), kind=kOutput, calls=%fused_computation.17 | convolution fusion | flops 226497024 | bytes 3145968 | tf_op jit(solution)/shard_map/tsn,sf->tfn/dot_general | solution.py:42
  77.5 0.5 copy.19
  78.0 0.8 fusion.6
  78.9 0.7 gather_fusion.1
  79.6 0.6 convolution_convert_fusion
  80.2 0.6 convert_element_type.26
  80.8 9.9 %fusion = bf16[16,4096]{1,0:T(8,128)(2,1)S(1)} fusion(bf16[48,4096]{1,0:T(8,128)(2,1)S(1)} %convert_element_type.26), kind=kCustom, calls=%all-reduce-scatter | all-reduce-scatter fusion | flops 262145 | bytes 524800
  90.8 4.4 %collective-permute-start = (bf16[12,4096]{1,0:T(8,128)(2,1)S(1)}, bf16[12,4096]{1,0:T(8,128)(2,1)S(1)}, u32[]{:S(2)}, u32[]{:S(2)}) collective-permute-start(bf16[12,4096]{1,0:T(8,128)(2,1)S(1)} %slice.18), channel_id=1, source_target_pairs={{0,1},{1,2},{2,3},{4,5},{5,6},{6,7},{8,9},{9,10},{10,11},{12,13},{... | collective-permute-start | bytes 294920
  95.2 1.2 %copy.21 = bf16[128,3072]{1,0:T(8,128)(2,1)} copy(bf16[128,3072]{0,1:T(8,128)(2,1)S(1)} %get-tuple-element.13) | data formatting | bytes 1572864
  96.3 0.8 collective-permute-done
  97.1 0.3 concatenate
  97.4 0.7 fusion.22
  (8 shorter events, 0.1 us)
Async XLA Ops:
  7.2 26.2 %copy-start = (bf16[128,3072]{1,0:T(8,128)(2,1)S(1)}, bf16[128,3072]{1,0:T(8,128)(2,1)}, u32[]{:S(2)}) copy-start(bf16[128,3072]{1,0:T(8,128)(2,1)} %param.9) | copy-start | bytes 2359300
  7.2 65.3 %all-gather.2.cloned.1.call-start = ((), (), s32[]{:S(2)}) async-start(), calls=%async_computation | async-start | bytes 3538944 | tf_op jit(solution)/shard_map/all_gather | solution.py:22
  90.8 6.3 %collective-permute-start = (bf16[12,4096]{1,0:T(8,128)(2,1)S(1)}, bf16[12,4096]{1,0:T(8,128)(2,1)S(1)}, u32[]{:S(2)}, u32[]{:S(2)}) collective-permute-start(bf16[12,4096]{1,0:T(8,128)(2,1)S(1)} %slice.18), channel_id=1, source_target_pairs={{0,1},{1,2},{2,3},{4,5},{5,6},{6,7},{8,9},{9,10},{10,11},{12,13},{... | collective-permute-start | bytes 294920
Sparse Core Ops, SparseCore 0:
  10.8 61.6 all-gather.1
where the time goes:
time: 105 us
  waiting for transfers between devices  35.6 us (34%)
  blocking collectives  28.9 us (28%)
  between operations  15.5 us (15%)
  local copies, waits for them, and re-layouts  12.8 us (12%)
  other arithmetic  4.89 us (5%)
  starting transfers between devices  4.39 us (4%)
  matrix products  3.01 us (3%)
    all_gather x1, waiting for transfers between devices, body(): features = lax.all_gather(activations, 'row', axis=1, tiled=True)  34.8 us
    unnamed x2, blocking collectives  15.1 us
    all_gather x1, blocking collectives, body(): lax.all_gather(weight_tiles, 'col', axis=0, tiled=True)  7.49 us
    all_gather x1, blocking collectives, body(): lax.all_gather(tile_ids, 'col', axis=0, tiled=True)  6.31 us
    unnamed x10, local copies, waits for them, and re-layouts  5.86 us
    unnamed x1, starting transfers between devices  4.35 us
    gather x1, local copies, waits for them, and re-layouts, body(): jnp.take(features.reshape(tok_rows, width // TILE, TILE), d_tile, axis=1)  2.58 us
    lt x1, other arithmetic, body(): live = position < slot_counts.reshape(columns)[owner]  2.54 us
  transfers between devices with their start and end apart: 2, of which 2 were waited for; matrix products, arithmetic and copies ran while one was open for 9% of the time, Pallas kernels for 0%

commit v1 on v0

v1 whole, which is shorter than its diff:
```python
import functools

import jax
import jax.numpy as jnp
from jax import lax
from jax.experimental import pallas as pl
from jax.experimental.pallas import tpu as pltpu
from jax.sharding import PartitionSpec as P

TILE = 64
LANES = 128
MESH = pl.DeviceIdType.MESH


def gelu_parts(pre):
    cumul = 0.5 * (1.0 + lax.erf(pre * 0.7071067811865476))
    density = jnp.exp(-0.5 * pre * pre) * 0.3989422804014327
    return (cumul, density)


def kernel(
    n_row, n_col, per_col,
    xt_ref, w_ref, ids_ref, cnt_ref, up_ref, out_ref, grad_ref,
    xg, sendx, recvx, wbuf, idsrc, idq, idc, sidq, sidc, pre, prod, g, dsend, drecv,
    xg_s, xg_r, ic_s, ic_r, iq_s, iq_r, w_s, w_r, xz_s, xz_r, d_s, d_r, loc,
):
    cap = ids_ref.shape[0]
    half = cap // 2
    group = n_row // n_col
    line = n_col
    own_tiles = xt_ref.shape[0]
    n_pair = pre.shape[0]
    col = lax.axis_index("col")
    row = lax.axis_index("row")
    z = row // group
    x = lax.rem(row, group)

    def member(k):
        return lax.rem(x + k, group)

    def at_line(k):
        return lax.rem(z + k, line)

    def at_col(k):
        return lax.rem(col + k, n_col)

    barrier = pltpu.get_barrier_semaphore()
    for k in range(1, group):
        pl.semaphore_signal(barrier, inc=1, device_id={"row": z * group + member(k)}, device_id_type=MESH)
    for k in range(1, line):
        pl.semaphore_signal(barrier, inc=1, device_id={"row": at_line(k) * group + x}, device_id_type=MESH)
    for k in range(1, n_col):
        pl.semaphore_signal(barrier, inc=1, device_id={"col": at_col(k)}, device_id_type=MESH)

    lane8 = lax.broadcasted_iota(jnp.int32, (8, LANES), 1)
    packed = jnp.where(lane8 == cap, cnt_ref[0], 0)
    for s in range(cap):
        packed = jnp.where(lane8 == s, ids_ref[s], packed)
    idsrc[...] = packed
    idc[col] = packed
    wbuf[col] = w_ref[...]
    pl.semaphore_wait(barrier, group + line + n_col - 3)

    def remote(src, dst, send, recv, target):
        return pltpu.make_async_remote_copy(
            src_ref=src, dst_ref=dst, send_sem=send, recv_sem=recv, device_id=target, device_id_type=MESH
        )

    def ids_col(k, owner):
        return remote(idsrc, idc.at[owner], ic_s.at[k], ic_r.at[owner], {"col": at_col(k)})

    def ids_line(k, owner):
        to = at_line(k)
        return remote(idc.at[to], idq.at[owner], iq_s.at[k], iq_r.at[owner], {"row": to * group + x})

    def w_col(k, owner):
        return remote(w_ref, wbuf.at[owner], w_s.at[k], w_r.at[owner], {"col": at_col(k)})

    def x_group(k, owner):
        return remote(
            xt_ref, xg.at[pl.ds(owner * own_tiles, own_tiles)], xg_s.at[k], xg_r.at[owner],
            {"row": z * group + member(k)},
        )

    def x_line(k, owner):
        to = at_line(k)
        return remote(sendx.at[to], recvx.at[owner], xz_s.at[k], xz_r.at[owner], {"row": to * group + x})

    def d_col(k, owner):
        to = at_col(k)
        return remote(dsend.at[to], drecv.at[owner], d_s.at[k], d_r.at[owner], {"col": to})

    for k in range(1, n_col):
        ids_col(k, col).start()
    for k in range(1, group):
        x_group(k, x).start()
    for k in range(1, n_col):
        w_col(k, col).start()
    xg[pl.ds(x * own_tiles, own_tiles)] = xt_ref[...]

    for k in range(1, n_col):
        ids_col(k, at_col(k)).wait_recv()
    for k in range(1, line):
        ids_line(k, z).start()
    idq[z] = idc[z]
    pre[...] = jnp.zeros_like(pre)
    for k in range(1, line):
        ids_line(k, at_line(k)).wait_recv()
    copy_q = pltpu.make_async_copy(idq, sidq, loc.at[0])
    copy_c = pltpu.make_async_copy(idc, sidc, loc.at[1])
    copy_q.start()
    copy_c.start()
    copy_q.wait()
    copy_c.wait()

    for k in range(1, group):
        x_group(k, member(k)).wait_recv()
    for k in range(line - 1, 0, -1):
        to = at_line(k)
        for s in range(cap):
            sendx[to, s] = xg[sidq[to, 0, s] // per_col]
        x_line(k, z).start()
    for s in range(cap):
        recvx[z, s] = xg[sidq[z, 0, s] // per_col]
    for k in range(1, n_col):
        w_col(k, at_col(k)).wait_recv()

    lane_half = lax.broadcasted_iota(jnp.int32, (TILE, LANES), 1) // TILE

    def add_block(b):
        count = sidc[b, 0, cap]
        places = []
        for s in range(cap):
            f = lax.rem(sidc[b, 0, s], per_col)
            places.append(jnp.where(s < count, f // 2, -1))
            both = jnp.where(lane_half == s // half, wbuf[b, s % half].astype(jnp.float32), 0.0)
            both = both + pltpu.roll(both, TILE, 1)
            placed = jnp.where(lane_half == lax.rem(f, 2), both, 0.0).astype(jnp.bfloat16)
            prod[s] = lax.dot_general(
                recvx[b, s], placed, (((0,), (0,)), ((), ())), preferred_element_type=jnp.float32
            )

        def add_pair(p, carry):
            total = pre[p]
            for s in range(cap):
                total = total + prod[s] * jnp.where(places[s] == p, 1.0, 0.0)
            pre[p] = total
            return carry

        lax.fori_loop(0, n_pair, add_pair, 0)

    add_block(z)

    def later_block(k, carry):
        b = at_line(k)
        x_line(k, b).wait_recv()
        add_block(b)
        return carry

    lax.fori_loop(1, line, later_block, 0)

    for p in range(n_pair):
        lanes = slice(p * LANES, (p + 1) * LANES)
        v = pre[p]
        cumul, density = gelu_parts(v)
        out_ref[:, lanes] = (v * cumul).astype(jnp.bfloat16)
        g[p] = (up_ref[:, lanes].astype(jnp.float32) * (cumul + v * density)).astype(jnp.bfloat16)

    def terms(b):
        for j in range(half):
            parts = []
            for s in (j, j + half):
                f = lax.rem(sidc[b, 0, s], per_col)
                r = jnp.dot(recvx[b, s], g[f // 2], preferred_element_type=jnp.float32)
                r = jnp.where(lane_half == lax.rem(f, 2), r, 0.0)
                parts.append(r + pltpu.roll(r, TILE, 1))
            dsend[b, j] = jnp.where(lane_half == 0, parts[0], parts[1]).astype(jnp.bfloat16)

    def send_terms(k, carry):
        terms(at_col(k))
        d_col(k, col).start()
        return carry

    lax.fori_loop(1, n_col, send_terms, 0)
    terms(col)
    for k in range(1, n_col):
        d_col(k, at_col(k)).wait_recv()
    own_count = cnt_ref[0]
    for j in range(half):
        total = dsend[col, j].astype(jnp.float32)
        for k in range(1, n_col):
            total = total + drecv[at_col(k), j].astype(jnp.float32)
        grad_ref[j] = jnp.where(lane_half * half + j < own_count, total, 0.0).astype(jnp.bfloat16)

    for k in range(1, group):
        x_group(k, x).wait_send()
    for k in range(1, line):
        ids_line(k, z).wait_send()
        x_line(k, z).wait_send()
    for k in range(1, n_col):
        ids_col(k, col).wait_send()
        w_col(k, col).wait_send()
        d_col(k, col).wait_send()


def body(activations, weight_tiles, tile_ids, tile_counts, upstream):
    n_row, n_col = lax.axis_size("row"), lax.axis_size("col")
    group = n_row // n_col
    tok, own_width = activations.shape
    ff_local = upstream.shape[1]
    per_col = ff_local // TILE
    cap = weight_tiles.shape[2]
    half = cap // 2
    own_tiles = own_width // TILE
    xt = activations.T.reshape(own_tiles, TILE, tok)
    w = weight_tiles.reshape(2, half, TILE, TILE).transpose(1, 2, 0, 3).reshape(half, TILE, 2 * TILE)
    bf16, f32, i32 = jnp.bfloat16, jnp.float32, jnp.int32
    vmem = pl.BlockSpec(memory_space=pltpu.VMEM)
    smem = pl.BlockSpec(memory_space=pltpu.SMEM)
    dma = pltpu.SemaphoreType.DMA
    n_pair = ff_local // LANES
    output, grad = pl.pallas_call(
        functools.partial(kernel, n_row, n_col, per_col),
        out_shape=(
            jax.ShapeDtypeStruct((tok, ff_local), bf16),
            jax.ShapeDtypeStruct((half, TILE, LANES), bf16),
        ),
        in_specs=[vmem, vmem, smem, smem, vmem],
        out_specs=(vmem, vmem),
        scratch_shapes=[
            pltpu.VMEM((group * own_tiles, TILE, tok), bf16),
            pltpu.VMEM((n_col, cap, TILE, tok), bf16),
            pltpu.VMEM((n_col, cap, TILE, tok), bf16),
            pltpu.VMEM((n_col, half, TILE, LANES), bf16),
            pltpu.VMEM((8, LANES), i32),
            pltpu.VMEM((n_col, 8, LANES), i32),
            pltpu.VMEM((n_col, 8, LANES), i32),
            pltpu.SMEM((n_col, 8, LANES), i32),
            pltpu.SMEM((n_col, 8, LANES), i32),
            pltpu.VMEM((n_pair, tok, LANES), f32),
            pltpu.VMEM((cap, tok, LANES), f32),
            pltpu.VMEM((n_pair, tok, LANES), bf16),
            pltpu.VMEM((n_col, half, TILE, LANES), bf16),
            pltpu.VMEM((n_col, half, TILE, LANES), bf16),
            dma((group,)), dma((group,)),
            dma((n_col,)), dma((n_col,)),
            dma((n_col,)), dma((n_col,)),
            dma((n_col,)), dma((n_col,)),
            dma((n_col,)), dma((n_col,)),
            dma((n_col,)), dma((n_col,)),
            dma((2,)),
        ],
        compiler_params=pltpu.CompilerParams(
            collective_id=0, has_side_effects=True, vmem_limit_bytes=40 * 1024 * 1024
        ),
    )(xt, w, tile_ids.reshape(cap), tile_counts.reshape(1), upstream)
    grad = grad.reshape(half, TILE, 2, TILE).transpose(2, 0, 1, 3)
    return (output, grad.reshape(1, 1, cap, TILE * TILE))


def solution(mesh):
    return jax.shard_map(
        body,
        mesh=mesh,
        in_specs=(
            P("col", "row"),
            P("col", "row", None, None),
            P("col", "row", None),
            P("col", "row"),
            P("col", "row"),
        ),
        out_specs=(P("col", "row"), P("col", "row", None, None)),
        check_vma=False,
    )
```

time: 105 us -> 49.7 us (0.47)
  Pallas kernels: 0 us -> 43.8 us
  waiting for transfers between devices: 35.6 us -> 0 us
  blocking collectives: 28.9 us -> 0 us
  between operations: 15.5 us -> 1.36 us
  local copies, waits for them, and re-layouts: 12.8 us -> 4.33 us
  other arithmetic: 4.89 us -> 0 us
  starting transfers between devices: 4.39 us -> 0 us
  matrix products: 3.01 us -> 0 us
    pallas_call x0 -> x1, Pallas kernels: none -> 43.8 us  [body(): pl.pallas_call(functools.partial(kernel, n_row, n_col, per_col), out_shap...]
    all_gather x1 -> x0, waiting for transfers between devices: 34.8 us -> none  [body(): features = lax.all_gather(activations, 'row', axis=1, tiled=True)]
    unnamed x2 -> x0, blocking collectives: 15.1 us -> none
    all_gather x2 -> x0, blocking collectives: 13.8 us -> none  [the longest x1 7.49 us: body(): lax.all_gather(weight_tiles, 'col', axis=0, tiled=True)]
    unnamed x1 -> x0, starting transfers between devices: 4.35 us -> none
    unnamed x10 -> x7, local copies, waits for them, and re-layouts: 5.86 us -> 1.6 us
    gather x3 -> x0, local copies, waits for them, and re-layouts: 3.95 us -> none  [the longest x1 2.58 us: body(): jnp.take(features.reshape(tok_rows, width // TILE, TILE), d_tile, axis=1)]
    dot_general x3 -> x0, matrix products: 3.01 us -> none  [the longest x1 1.9 us: body(): jnp.einsum('tsn,sf->tfn', partial_value, placing, precision=lax.Precision...]
  transfers between devices with their start and end apart: 2 -> 0, of which waited for: 2 -> 0; matrix products, arithmetic and copies ran while one was open for 9% -> 0% of each run, Pallas kernels for 0% -> 0%
where the time goes in v1:
time: 49.7 us; the launch traced here: 49.5 us
  Pallas kernels  43.8 us (88%)
  local copies, waits for them, and re-layouts  4.33 us (9%)
  between operations  1.36 us (3%)
    pallas_call x1, Pallas kernels, body(): pl.pallas_call(functools.partial(kernel, n_row, n_col, per_col), out_shap...  43.8 us
    unnamed x7, local copies, waits for them, and re-layouts  1.6 us
    reshape x3, local copies, waits for them, and re-layouts, body(): weight_tiles.reshape(2, half, TILE, TILE).transpose(1, 2, 0, 3)  1.51 us

profile of v1, /device:TPU:1, one launch (start us, length us, event | category | flops | bytes accessed | tf_op | source)
XLA Modules:
  0.0 49.5 jit_solution(16080408279555663720)
XLA Ops:
  1.3 0.0 copy-start.2
  1.3 1.2 %reshape.26 = bf16[2,6,64,64]{3,2,1,0:T(8,128)(2,1)S(1)} reshape(bf16[1,1,12,4096]{3,2,1,0:T(8,128)(2,1)} %param.6) | data formatting | bytes 196608 | tf_op jit(solution)/shard_map/reshape | solution.py:216
  2.5 0.0 copy-start
  2.5 0.2 copy.11
  2.7 0.1 reshape.27.w_ref
  2.8 0.0 copy-done.2
  2.8 0.2 copy.7
  3.1 0.0 copy-start.1
  3.1 0.5 %copy-done = bf16[128,3072]{1,0:T(8,128)(2,1)S(1)} copy-done((bf16[128,3072]{1,0:T(8,128)(2,1)S(1)}, bf16[128,3072]{1,0:T(8,128)(2,1)}, u32[]{:S(2)}) %copy-start) | copy-done | bytes 786456
  3.6 0.2 copy-done.1
  3.8 43.8 %shard_map.68 = (bf16[128,3072]{1,0:T(8,128)(2,1)S(1)}, bf16[6,64,128]{2,1,0:T(8,128)(2,1)S(1)}) custom-call(bf16[24,64,128]{2,1,0:T(8,128)(2,1)S(1)} %bitcast.11, bf16[6,64,128]{2,1,0:T(8,128)(2,1)S(1)} %reshape.27.w_ref, s32[12]{0:T(128)S(1)} %bitcast.12, s32[1]{0:T(128)} %bitcast.10.cnt_ref, bf16[128,3072]{1,0:T(8,128)(2,1)S(1)} %copy-done), custom_call_target="tpu_custom_call" | custom-call | tf_op jit(solution)/shard_map/pallas_call | solution.py:222
  47.6 0.1 reshape.30
  47.8 0.8 %reshape.31 = bf16[1,1,12,4096]{3,2,1,0:T(8,128)(2,1)} reshape(bf16[2,6,64,64]{3,2,1,0:T(8,128)(2,1)S(1)} %copy.9) | data formatting | bytes 196608 | tf_op jit(solution)/shard_map/reshape | solution.py:258
  48.6 0.9 %copy.14 = bf16[128,3072]{1,0:T(8,128)(2,1)} copy(bf16[128,3072]{1,0:T(8,128)(2,1)S(1)} %get-tuple-element.8) | data formatting | bytes 1572864
  (1 shorter events, 0.0 us)
Async XLA Ops:
  1.3 1.6 %copy-start.2 = (bf16[128,1536]{1,0:T(8,128)(2,1)S(1)}, bf16[128,1536]{1,0:T(8,128)(2,1)}, u32[]{:S(2)}) copy-start(bf16[128,1536]{1,0:T(8,128)(2,1)} %param.5) | copy-start | bytes 1179652
  2.5 1.1 %copy-start = (bf16[128,3072]{1,0:T(8,128)(2,1)S(1)}, bf16[128,3072]{1,0:T(8,128)(2,1)}, u32[]{:S(2)}) copy-start(bf16[128,3072]{1,0:T(8,128)(2,1)} %up_ref.1) | copy-start | bytes 2359300
  3.1 0.7 %copy-start.1 = (s32[1,1,12]{2,1,0:T(1,128)S(1)}, s32[1,1,12]{2,1,0:T(1,128)}, u32[]{:S(2)}) copy-start(s32[1,1,12]{2,1,0:T(1,128)} %param.7) | copy-start | bytes 148

commit v2 on v1

v2 whole, which is shorter than its diff:
```python
import functools

import jax
import jax.numpy as jnp
from jax import lax
from jax.experimental import pallas as pl
from jax.experimental.pallas import tpu as pltpu
from jax.sharding import PartitionSpec as P

TILE = 64
LANES = 128
CHUNKS = 4
UNROLL = 3
MESH = pl.DeviceIdType.MESH


def gelu_parts(pre):
    cumul = 0.5 * (1.0 + lax.erf(pre * 0.7071067811865476))
    density = jnp.exp(-0.5 * pre * pre) * 0.3989422804014327
    return (cumul, density)


def kernel(
    n_row, n_col, per_col,
    x_ref, w_ref, ids_ref, cnt_ref, up_ref, out_ref, grad_ref, *scratch,
):
    xg, scratch = scratch[:CHUNKS], scratch[CHUNKS:]
    (
        sendx, recvx, wbuf, wpl, idsrc, idq, idc, sidq, sidc, table, stable, prod, run, g, dw, dsend, drecv,
        xg_s, xg_r, ic_s, ic_r, iq_s, iq_r, w_s, w_r, xz_s, xz_r, d_s, d_r, loc,
    ) = scratch
    cap = ids_ref.shape[0]
    half = cap // 2
    slots = n_col * cap
    group = n_row // n_col
    line = n_col
    chunks = len(xg)
    all_tiles, packed_rows, _ = xg[0].shape
    tc = 2 * packed_rows
    own_tiles = all_tiles // group
    n_pair = g.shape[0]
    col = lax.axis_index("col")
    row = lax.axis_index("row")
    z = row // group
    x = lax.rem(row, group)

    def member(k):
        return lax.rem(x + k, group)

    def at_line(k):
        return lax.rem(z + k, line)

    def at_col(k):
        return lax.rem(col + k, n_col)

    barrier = pltpu.get_barrier_semaphore()
    for k in range(1, group):
        pl.semaphore_signal(barrier, inc=1, device_id={"row": z * group + member(k)}, device_id_type=MESH)
    for k in range(1, line):
        pl.semaphore_signal(barrier, inc=1, device_id={"row": at_line(k) * group + x}, device_id_type=MESH)
    for k in range(1, n_col):
        pl.semaphore_signal(barrier, inc=1, device_id={"col": at_col(k)}, device_id_type=MESH)

    lane8 = lax.broadcasted_iota(jnp.int32, (8, LANES), 1)
    packed = jnp.where(lane8 == cap, cnt_ref[0], 0)
    for s in range(cap):
        packed = jnp.where(lane8 == s, ids_ref[s], packed)
    idsrc[...] = packed
    idc[col] = packed
    wbuf[col] = w_ref[...]

    def pack(c):
        for t in range(own_tiles):
            lanes = slice(t * TILE, (t + 1) * TILE)
            top = x_ref[c * tc : c * tc + packed_rows, lanes].astype(jnp.float32)
            bottom = x_ref[c * tc + packed_rows : (c + 1) * tc, lanes].astype(jnp.float32)
            xg[c][x * own_tiles + t] = jnp.concatenate([top, bottom], axis=1).astype(jnp.bfloat16)

    pack(0)
    pl.semaphore_wait(barrier, group + line + n_col - 3)

    def remote(src, dst, send, recv, target):
        return pltpu.make_async_remote_copy(
            src_ref=src, dst_ref=dst, send_sem=send, recv_sem=recv, device_id=target, device_id_type=MESH
        )

    def ids_col(k, owner):
        return remote(idsrc, idc.at[owner], ic_s.at[k], ic_r.at[owner], {"col": at_col(k)})

    def ids_line(k, owner):
        to = at_line(k)
        return remote(idc.at[to], idq.at[owner], iq_s.at[k], iq_r.at[owner], {"row": to * group + x})

    def w_col(k, owner):
        return remote(w_ref, wbuf.at[owner], w_s.at[k], w_r.at[owner], {"col": at_col(k)})

    def x_group(c, k, owner):
        mine = xg[c].at[pl.ds(x * own_tiles, own_tiles)]
        theirs = xg[c].at[pl.ds(owner * own_tiles, own_tiles)]
        return remote(mine, theirs, xg_s.at[c, k], xg_r.at[c, owner], {"row": z * group + member(k)})

    def x_line(c, k, owner):
        to = at_line(k)
        return remote(
            sendx.at[c, to], recvx.at[c, owner], xz_s.at[c, k], xz_r.at[c, owner], {"row": to * group + x}
        )

    def d_col(k, owner):
        to = at_col(k)
        return remote(dsend.at[to], drecv.at[owner], d_s.at[k], d_r.at[owner], {"col": to})

    for k in range(1, n_col):
        ids_col(k, col).start()
    for k in range(1, group):
        x_group(0, k, x).start()
    for k in range(1, n_col):
        w_col(k, col).start()
    for c in range(1, chunks):
        pack(c)
        for k in range(1, group):
            x_group(c, k, x).start()

    for k in range(1, n_col):
        ids_col(k, at_col(k)).wait_recv()
    for k in range(1, line):
        ids_line(k, z).start()
    idq[z] = idc[z]
    copy_c = pltpu.make_async_copy(idc, sidc, loc.at[1])
    copy_c.start()
    for k in range(1, line):
        ids_line(k, at_line(k)).wait_recv()
    copy_q = pltpu.make_async_copy(idq, sidq, loc.at[0])
    copy_q.start()
    copy_c.wait()
    copy_q.wait()

    for c in range(chunks):
        for k in range(1, group):
            x_group(c, k, member(k)).wait_recv()
        for k in range(line - 1, 0, -1):
            to = at_line(k)
            for s in range(cap):
                sendx[c, to, s] = xg[c][sidq[to, 0, s] // per_col]
            x_line(c, k, z).start()
        for s in range(cap):
            recvx[c, z, s] = xg[c][sidq[z, 0, s] // per_col]

    width = table.shape[1]
    lanes_s = lax.broadcasted_iota(jnp.int32, (slots, width), 1)
    rows_s = lax.broadcasted_iota(jnp.int32, (slots, width), 0)
    key_row = jnp.full((1, width), per_col + 1, jnp.int32) * slots + slots
    key_col = jnp.zeros((slots, width), jnp.int32)
    lane1 = lax.broadcasted_iota(jnp.int32, (1, width), 1)
    for s in range(slots):
        b, j = s // cap, s % cap
        f = jnp.where(j < sidc[b, 0, cap], lax.rem(sidc[b, 0, j], per_col), per_col)
        key_row = jnp.where(lane1 == s, f * slots + s, key_row)
        key_col = jnp.where(rows_s == s, f, key_col)
    ahead = jnp.where(key_row < key_col * slots + rows_s, 1, 0)
    rank = jnp.sum(ahead, axis=1, keepdims=True)
    here = jnp.where(rank == lanes_s, 1, 0)
    table[0:1, :] = jnp.sum(here * rows_s, axis=0, keepdims=True)
    table[1:2, :] = jnp.sum(here * key_col, axis=0, keepdims=True)
    upto = jnp.sum(jnp.where(key_col <= lanes_s, 1, 0), axis=0, keepdims=True)
    some = jnp.sum(jnp.where(key_col == lanes_s, 1, 0), axis=0, keepdims=True)
    table[2:3, :] = jnp.where(some > 0, upto - 1, slots)
    table[3:8, :] = jnp.zeros((5, width), jnp.int32)
    copy_t = pltpu.make_async_copy(table, stable, loc.at[0])
    copy_t.start()
    copy_t.wait()

    for k in range(1, n_col):
        w_col(k, at_col(k)).wait_recv()

    lane_half = lax.broadcasted_iota(jnp.int32, (TILE, LANES), 1) // TILE

    def place_weights(b, carry):
        for s in range(cap):
            f = lax.rem(sidc[b, 0, s], per_col)
            both = jnp.where(lane_half == s // half, wbuf[b, s % half].astype(jnp.float32), 0.0)
            both = both + pltpu.roll(both, TILE, 1)
            placed = jnp.where(lane_half == lax.rem(f, 2), both, 0.0).astype(jnp.bfloat16)
            wpl[b * cap + s, :TILE] = placed
            wpl[b * cap + s, TILE:] = placed
        return carry

    lax.fori_loop(0, n_col, place_weights, 0)
    run[slots] = jnp.zeros((tc, LANES), jnp.float32)

    packed_half = lax.broadcasted_iota(jnp.int32, (packed_rows, LANES), 1) // TILE
    first = jnp.where(packed_half == 0, 1.0, 0.0).astype(jnp.bfloat16)
    second = jnp.where(packed_half == 1, 1.0, 0.0).astype(jnp.bfloat16)

    def spread(c, b, s):
        tile = recvx[c, b, s]
        return jnp.concatenate([tile * first, tile * second], axis=0)

    def products(c, b):
        for s in range(cap):
            prod[b * cap + s] = jnp.dot(spread(c, b, s), wpl[b * cap + s], preferred_element_type=jnp.float32)

    def hidden(c):
        products(c, z)

        def later(k, carry):
            b = at_line(k)
            x_line(c, k, b).wait_recv()
            products(c, b)
            return carry

        lax.fori_loop(1, line, later, 0)

        def add_run(r, held):
            same = jnp.where(stable[1, r] == stable[1, jnp.maximum(r - 1, 0)], 1.0, 0.0)
            total = prod[stable[0, r]] + held * same
            run[r] = total
            return total

        lax.fori_loop(0, slots, add_run, jnp.zeros((tc, LANES), jnp.float32), unroll=4)

        rows = pl.ds(pl.multiple_of(c * tc, tc), tc)

        def gelu_pair(p, carry):
            lanes = pl.ds(pl.multiple_of(p * LANES, LANES), LANES)
            v = run[stable[2, 2 * p]] + run[stable[2, 2 * p + 1]]
            cumul, density = gelu_parts(v)
            out_ref[rows, lanes] = (v * cumul).astype(jnp.bfloat16)
            g[p] = (up_ref[rows, lanes].astype(jnp.float32) * (cumul + v * density)).astype(jnp.bfloat16)
            return carry

        lax.fori_loop(0, n_pair, gelu_pair, 0, unroll=UNROLL)

    def add_terms(c, b, first_chunk):
        for s in range(cap):
            f = lax.rem(sidc[b, 0, s], per_col)
            r = lax.dot_general(
                spread(c, b, s), g[f // 2], (((0,), (0,)), ((), ())), preferred_element_type=jnp.float32
            )
            term = r[:TILE] + r[TILE:]
            dw[b * cap + s] = term if first_chunk else dw[b * cap + s] + term

    def round_terms(b):
        for j in range(half):
            parts = []
            for s in (j, j + half):
                f = lax.rem(sidc[b, 0, s], per_col)
                r = jnp.where(lane_half == lax.rem(f, 2), dw[b * cap + s], 0.0)
                parts.append(r + pltpu.roll(r, TILE, 1))
            dsend[b, j] = jnp.where(lane_half == 0, parts[0], parts[1]).astype(jnp.bfloat16)

    def all_terms(c, first_chunk):
        def one(b, carry):
            add_terms(c, b, first_chunk)
            return carry

        lax.fori_loop(0, n_col, one, 0)

    hidden(0)
    if chunks > 1:
        all_terms(0, True)

        def middle(c, carry):
            hidden(c)
            all_terms(c, False)
            return carry

        lax.fori_loop(1, chunks - 1, middle, 0)
        hidden(chunks - 1)

    def send_terms(i, carry):
        k = 1 + lax.rem(n_col // 2 - 1 + i, n_col - 1)
        b = at_col(k)
        add_terms(chunks - 1, b, chunks == 1)
        round_terms(b)
        d_col(k, col).start()
        return carry

    lax.fori_loop(0, n_col - 1, send_terms, 0)
    add_terms(chunks - 1, col, chunks == 1)
    round_terms(col)
    for k in range(1, n_col):
        d_col(k, at_col(k)).wait_recv()
    own_count = cnt_ref[0]
    for j in range(half):
        total = dsend[col, j].astype(jnp.float32)
        for k in range(1, n_col):
            total = total + drecv[at_col(k), j].astype(jnp.float32)
        grad_ref[j] = jnp.where(lane_half * half + j < own_count, total, 0.0).astype(jnp.bfloat16)

    for c in range(chunks):
        for k in range(1, group):
            x_group(c, k, x).wait_send()
        for k in range(1, line):
            x_line(c, k, z).wait_send()
    for k in range(1, line):
        ids_line(k, z).wait_send()
    for k in range(1, n_col):
        ids_col(k, col).wait_send()
        w_col(k, col).wait_send()
        d_col(k, col).wait_send()


def body(activations, weight_tiles, tile_ids, tile_counts, upstream):
    n_row, n_col = lax.axis_size("row"), lax.axis_size("col")
    group = n_row // n_col
    tok, own_width = activations.shape
    ff_local = upstream.shape[1]
    per_col = ff_local // TILE
    cap = weight_tiles.shape[2]
    half = cap // 2
    slots = n_col * cap
    own_tiles = own_width // TILE
    tc = tok // CHUNKS
    rows = tc // 2
    width = -(-max(slots, per_col) // LANES) * LANES
    w = weight_tiles.reshape(2, half, TILE, TILE).transpose(1, 2, 0, 3).reshape(half, TILE, 2 * TILE)
    bf16, f32, i32 = jnp.bfloat16, jnp.float32, jnp.int32
    vmem = pl.BlockSpec(memory_space=pltpu.VMEM)
    smem = pl.BlockSpec(memory_space=pltpu.SMEM)
    dma = pltpu.SemaphoreType.DMA
    n_pair = ff_local // LANES
    output, grad = pl.pallas_call(
        functools.partial(kernel, n_row, n_col, per_col),
        out_shape=(
            jax.ShapeDtypeStruct((tok, ff_local), bf16),
            jax.ShapeDtypeStruct((half, TILE, LANES), bf16),
        ),
        in_specs=[vmem, vmem, smem, smem, vmem],
        out_specs=(vmem, vmem),
        scratch_shapes=[
            *[pltpu.VMEM((group * own_tiles, rows, LANES), bf16) for _ in range(CHUNKS)],
            pltpu.VMEM((CHUNKS, n_col, cap, rows, LANES), bf16),
            pltpu.VMEM((CHUNKS, n_col, cap, rows, LANES), bf16),
            pltpu.VMEM((n_col, half, TILE, LANES), bf16),
            pltpu.VMEM((slots, 2 * TILE, LANES), bf16),
            pltpu.VMEM((8, LANES), i32),
            pltpu.VMEM((n_col, 8, LANES), i32),
            pltpu.VMEM((n_col, 8, LANES), i32),
            pltpu.SMEM((n_col, 8, LANES), i32),
            pltpu.SMEM((n_col, 8, LANES), i32),
            pltpu.VMEM((8, width), i32),
            pltpu.SMEM((8, width), i32),
            pltpu.VMEM((slots, tc, LANES), f32),
            pltpu.VMEM((slots + 1, tc, LANES), f32),
            pltpu.VMEM((n_pair, tc, LANES), bf16),
            pltpu.VMEM((slots, TILE, LANES), f32),
            pltpu.VMEM((n_col, half, TILE, LANES), bf16),
            pltpu.VMEM((n_col, half, TILE, LANES), bf16),
            dma((CHUNKS, group)), dma((CHUNKS, group)),
            dma((n_col,)), dma((n_col,)),
            dma((n_col,)), dma((n_col,)),
            dma((n_col,)), dma((n_col,)),
            dma((CHUNKS, n_col)), dma((CHUNKS, n_col)),
            dma((n_col,)), dma((n_col,)),
            dma((2,)),
        ],
        compiler_params=pltpu.CompilerParams(
            collective_id=0, has_side_effects=True, vmem_limit_bytes=48 * 1024 * 1024
        ),
    )(activations, w, tile_ids.reshape(cap), tile_counts.reshape(1), upstream)
    grad = grad.reshape(half, TILE, 2, TILE).transpose(2, 0, 1, 3)
    return (output, grad.reshape(1, 1, cap, TILE * TILE))


def solution(mesh):
    return jax.shard_map(
        body,
        mesh=mesh,
        in_specs=(
            P("col", "row"),
            P("col", "row", None, None),
            P("col", "row", None),
            P("col", "row"),
            P("col", "row"),
        ),
        out_specs=(P("col", "row"), P("col", "row", None, None)),
        check_vma=False,
    )
```

time: 49.7 us -> 46.4 us (0.934)
  Pallas kernels: 43.8 us -> 39.9 us
  local copies, waits for them, and re-layouts: 4.33 us -> 4.85 us
    pallas_call x1, Pallas kernels: 43.8 us -> 39.9 us  [body(): pl.pallas_call(functools.partial(kernel, n_row, n_col, per_col), out_shap...]
    unnamed x7, local copies, waits for them, and re-layouts: 1.6 us -> 2.39 us
where the time goes in v2:
time: 46.4 us; the launch traced here: 46.2 us
  Pallas kernels  39.9 us (86%)
  local copies, waits for them, and re-layouts  4.85 us (10%)
  between operations  1.42 us (3%)
    pallas_call x1, Pallas kernels, body(): pl.pallas_call(functools.partial(kernel, n_row, n_col, per_col), out_shap...  39.9 us
    unnamed x7, local copies, waits for them, and re-layouts  2.39 us
    reshape x3, local copies, waits for them, and re-layouts, body(): weight_tiles.reshape(2, half, TILE, TILE).transpose(1, 2, 0, 3)  1.46 us

profile of v2, /device:TPU:1, one launch (start us, length us, event | category | flops | bytes accessed | tf_op | source)
XLA Modules:
  0.0 46.2 jit_solution(15080074525866607035)
XLA Ops:
  0.6 0.0 copy-start
  1.4 1.1 %reshape.22 = bf16[2,6,64,64]{3,2,1,0:T(8,128)(2,1)S(1)} reshape(bf16[1,1,12,4096]{3,2,1,0:T(8,128)(2,1)} %param.6) | data formatting | bytes 196608 | tf_op jit(solution)/shard_map/reshape | solution.py:316
  2.5 0.2 copy.10
  2.7 0.0 copy-start.2
  2.7 0.1 reshape.23.w_ref
  2.9 0.0 copy-done
  2.9 0.5 %copy-done.2 = s32[1,1,12]{2,1,0:T(1,128)S(1)} copy-done((s32[1,1,12]{2,1,0:T(1,128)S(1)}, s32[1,1,12]{2,1,0:T(1,128)}, u32[]{:S(2)}) %copy-start.2) | copy-done | bytes 72
  3.4 0.0 copy-start.1
  3.4 1.0 %copy-done.1 = bf16[128,1536]{1,0:T(8,128)(2,1)S(1)} copy-done((bf16[128,1536]{1,0:T(8,128)(2,1)S(1)}, bf16[128,1536]{1,0:T(8,128)(2,1)}, u32[]{:S(2)}) %copy-start.1) | copy-done | bytes 393240
  4.4 39.9 %shard_map.68 = (bf16[128,3072]{1,0:T(8,128)(2,1)S(1)}, bf16[6,64,128]{2,1,0:T(8,128)(2,1)S(1)}) custom-call(bf16[128,1536]{1,0:T(8,128)(2,1)S(1)} %copy-done.1, bf16[6,64,128]{2,1,0:T(8,128)(2,1)S(1)} %reshape.23.w_ref, s32[12]{0:T(128)S(1)} %bitcast.9, s32[1]{0:T(128)} %bitcast.8.cnt_ref, bf16[128,3072]{1,0:T(8,128)(2,1)S(1)} %copy-done), custom_call_target="tpu_custom_call" | custom-call | tf_op jit(solution)/shard_map/pallas_call | solution.py:322
  44.3 0.1 reshape.26
  44.5 0.8 %reshape.27 = bf16[1,1,12,4096]{3,2,1,0:T(8,128)(2,1)} reshape(bf16[2,6,64,64]{3,2,1,0:T(8,128)(2,1)S(1)} %copy.8) | data formatting | bytes 196608 | tf_op jit(solution)/shard_map/reshape | solution.py:362
  45.3 0.9 %copy.13 = bf16[128,3072]{1,0:T(8,128)(2,1)} copy(bf16[128,3072]{1,0:T(8,128)(2,1)S(1)} %get-tuple-element.8) | data formatting | bytes 1572864
  (1 shorter events, 0.0 us)
Async XLA Ops:
  0.6 2.2 %copy-start = (bf16[128,3072]{1,0:T(8,128)(2,1)S(1)}, bf16[128,3072]{1,0:T(8,128)(2,1)}, u32[]{:S(2)}) copy-start(bf16[128,3072]{1,0:T(8,128)(2,1)} %up_ref.1) | copy-start | bytes 2359300
  2.7 0.7 %copy-start.2 = (s32[1,1,12]{2,1,0:T(1,128)S(1)}, s32[1,1,12]{2,1,0:T(1,128)}, u32[]{:S(2)}) copy-start(s32[1,1,12]{2,1,0:T(1,128)} %param.7) | copy-start | bytes 148
  3.4 1.0 %copy-start.1 = (bf16[128,1536]{1,0:T(8,128)(2,1)S(1)}, bf16[128,1536]{1,0:T(8,128)(2,1)}, u32[]{:S(2)}) copy-start(bf16[128,1536]{1,0:T(8,128)(2,1)} %x_ref.1) | copy-start | bytes 1179652

commit v3 on v2

--- a/solution.py
+++ b/solution.py
@@ -22,11 +22,12 @@
 
 def kernel(
     n_row, n_col, per_col,
-    x_ref, w_ref, ids_ref, cnt_ref, up_ref, out_ref, grad_ref, *scratch,
+    x_hbm, w_ref, ids_ref, cnt_ref, up_hbm, out_ref, grad_ref, *scratch,
 ):
     xg, scratch = scratch[:CHUNKS], scratch[CHUNKS:]
     (
-        sendx, recvx, wbuf, wpl, idsrc, idq, idc, sidq, sidc, table, stable, prod, run, g, dw, dsend, drecv,
+        x_ref, up_ref, natural, mixed, wsrc, sendx, recvx, wbuf, wpl, xall, idsrc, idq, idc, sidq, sidc, table, stable,
+        prod, run, g, gt, dsend, drecv,
         xg_s, xg_r, ic_s, ic_r, iq_s, iq_r, w_s, w_r, xz_s, xz_r, d_s, d_r, loc,
     ) = scratch
     cap = ids_ref.shape[0]
@@ -53,6 +54,10 @@
     def at_col(k):
         return lax.rem(col + k, n_col)
 
+    copy_x = pltpu.make_async_copy(x_hbm, x_ref, loc.at[2])
+    copy_up = pltpu.make_async_copy(up_hbm, up_ref, loc.at[3])
+    copy_x.start()
+    copy_up.start()
     barrier = pltpu.get_barrier_semaphore()
     for k in range(1, group):
         pl.semaphore_signal(barrier, inc=1, device_id={"row": z * group + member(k)}, device_id_type=MESH)
@@ -67,7 +72,6 @@
         packed = jnp.where(lane8 == s, ids_ref[s], packed)
     idsrc[...] = packed
     idc[col] = packed
-    wbuf[col] = w_ref[...]
 
     def pack(c):
         for t in range(own_tiles):
@@ -76,6 +80,7 @@
             bottom = x_ref[c * tc + packed_rows : (c + 1) * tc, lanes].astype(jnp.float32)
             xg[c][x * own_tiles + t] = jnp.concatenate([top, bottom], axis=1).astype(jnp.bfloat16)
 
+    copy_x.wait()
     pack(0)
     pl.semaphore_wait(barrier, group + line + n_col - 3)
 
@@ -92,7 +97,7 @@
         return remote(idc.at[to], idq.at[owner], iq_s.at[k], iq_r.at[owner], {"row": to * group + x})
 
     def w_col(k, owner):
-        return remote(w_ref, wbuf.at[owner], w_s.at[k], w_r.at[owner], {"col": at_col(k)})
+        return remote(wsrc, wbuf.at[owner], w_s.at[k], w_r.at[owner], {"col": at_col(k)})
 
     def x_group(c, k, owner):
         mine = xg[c].at[pl.ds(x * own_tiles, own_tiles)]
@@ -113,8 +118,6 @@
         ids_col(k, col).start()
     for k in range(1, group):
         x_group(0, k, x).start()
-    for k in range(1, n_col):
-        w_col(k, col).start()
     for c in range(1, chunks):
         pack(c)
         for k in range(1, group):
@@ -127,6 +130,21 @@
     idq[z] = idc[z]
     copy_c = pltpu.make_async_copy(idc, sidc, loc.at[1])
     copy_c.start()
+
+    lane_half = lax.broadcasted_iota(jnp.int32, (TILE, LANES), 1) // TILE
+    low = lax.broadcasted_iota(jnp.int32, (TILE // 2, LANES), 1) < TILE
+    even, odd = pl.ds(0, TILE // 2, stride=2), pl.ds(1, TILE // 2, stride=2)
+    for j in range(TILE // 2):
+        natural[:, j, :] = w_ref[:, j * LANES : (j + 1) * LANES].astype(jnp.float32)
+    for j in range(half):
+        one, two = natural[j], natural[j + half]
+        mixed[even, :] = jnp.where(low, one, pltpu.roll(two, TILE, 1))
+        mixed[odd, :] = jnp.where(low, pltpu.roll(one, TILE, 1), two)
+        wsrc[j] = mixed[...].astype(jnp.bfloat16)
+    wbuf[col] = wsrc[...]
+    for k in range(1, n_col):
+        w_col(k, col).start()
+
     for k in range(1, line):
         ids_line(k, at_line(k)).wait_recv()
     copy_q = pltpu.make_async_copy(idq, sidq, loc.at[0])
@@ -172,8 +190,6 @@
     for k in range(1, n_col):
         w_col(k, at_col(k)).wait_recv()
 
-    lane_half = lax.broadcasted_iota(jnp.int32, (TILE, LANES), 1) // TILE
-
     def place_weights(b, carry):
         for s in range(cap):
             f = lax.rem(sidc[b, 0, s], per_col)
@@ -191,15 +207,17 @@
     first = jnp.where(packed_half == 0, 1.0, 0.0).astype(jnp.bfloat16)
     second = jnp.where(packed_half == 1, 1.0, 0.0).astype(jnp.bfloat16)
 
-    def spread(c, b, s):
-        tile = recvx[c, b, s]
-        return jnp.concatenate([tile * first, tile * second], axis=0)
+    def chunk_rows(c):
+        return pl.ds(pl.multiple_of(c * tc, tc), tc)
 
     def products(c, b):
         for s in range(cap):
-            prod[b * cap + s] = jnp.dot(spread(c, b, s), wpl[b * cap + s], preferred_element_type=jnp.float32)
-
-    def hidden(c):
+            tile = recvx[c, b, s]
+            spread = jnp.concatenate([tile * first, tile * second], axis=0)
+            xall[b * cap + s, chunk_rows(c)] = spread
+            prod[b * cap + s] = jnp.dot(spread, wpl[b * cap + s], preferred_element_type=jnp.float32)
+
+    def hidden(c, last):
         products(c, z)
 
         def later(k, carry):
@@ -218,66 +236,48 @@
 
         lax.fori_loop(0, slots, add_run, jnp.zeros((tc, LANES), jnp.float32), unroll=4)
 
-        rows = pl.ds(pl.multiple_of(c * tc, tc), tc)
+        rows = chunk_rows(c)
 
         def gelu_pair(p, carry):
             lanes = pl.ds(pl.multiple_of(p * LANES, LANES), LANES)
             v = run[stable[2, 2 * p]] + run[stable[2, 2 * p + 1]]
             cumul, density = gelu_parts(v)
             out_ref[rows, lanes] = (v * cumul).astype(jnp.bfloat16)
-            g[p] = (up_ref[rows, lanes].astype(jnp.float32) * (cumul + v * density)).astype(jnp.bfloat16)
+            g[p, rows] = (up_ref[rows, lanes].astype(jnp.float32) * (cumul + v * density)).astype(jnp.bfloat16)
+            if last:
+                both = g[p].astype(jnp.float32).T.astype(jnp.bfloat16)
+                gt[2 * p] = both[:TILE]
+                gt[2 * p + 1] = both[TILE:]
             return carry
 
         lax.fori_loop(0, n_pair, gelu_pair, 0, unroll=UNROLL)
 
-    def add_terms(c, b, first_chunk):
-        for s in range(cap):
-            f = lax.rem(sidc[b, 0, s], per_col)
-            r = lax.dot_general(
-                spread(c, b, s), g[f // 2], (((0,), (0,)), ((), ())), preferred_element_type=jnp.float32
-            )
-            term = r[:TILE] + r[TILE:]
-            dw[b * cap + s] = term if first_chunk else dw[b * cap + s] + term
-
-    def round_terms(b):
+    def terms(b):
         for j in range(half):
             parts = []
-            for s in (j, j + half):
-                f = lax.rem(sidc[b, 0, s], per_col)
-                r = jnp.where(lane_half == lax.rem(f, 2), dw[b * cap + s], 0.0)
-                parts.append(r + pltpu.roll(r, TILE, 1))
-            dsend[b, j] = jnp.where(lane_half == 0, parts[0], parts[1]).astype(jnp.bfloat16)
-
-    def all_terms(c, first_chunk):
-        def one(b, carry):
-            add_terms(c, b, first_chunk)
-            return carry
-
-        lax.fori_loop(0, n_col, one, 0)
-
-    hidden(0)
-    if chunks > 1:
-        all_terms(0, True)
-
-        def middle(c, carry):
-            hidden(c)
-            all_terms(c, False)
-            return carry
-
-        lax.fori_loop(1, chunks - 1, middle, 0)
-        hidden(chunks - 1)
+            for i in (j, j + half):
+                f = lax.rem(sidc[b, 0, i], per_col)
+                parts.append(jnp.dot(gt[f], xall[b * cap + i], preferred_element_type=jnp.float32))
+            turned = jnp.concatenate(parts, axis=0).T
+            dsend[b, j] = (turned[:TILE] + turned[TILE:]).astype(jnp.bfloat16)
+
+    copy_up.wait()
+
+    def early(c, carry):
+        hidden(c, False)
+        return carry
+
+    lax.fori_loop(0, chunks - 1, early, 0)
+    hidden(chunks - 1, True)
 
     def send_terms(i, carry):
         k = 1 + lax.rem(n_col // 2 - 1 + i, n_col - 1)
-        b = at_col(k)
-        add_terms(chunks - 1, b, chunks == 1)
-        round_terms(b)
+        terms(at_col(k))
         d_col(k, col).start()
         return carry
 
     lax.fori_loop(0, n_col - 1, send_terms, 0)
-    add_terms(chunks - 1, col, chunks == 1)
-    round_terms(col)
+    terms(col)
     for k in range(1, n_col):
         d_col(k, at_col(k)).wait_recv()
     own_count = cnt_ref[0]
@@ -285,7 +285,12 @@
         total = dsend[col, j].astype(jnp.float32)
         for k in range(1, n_col):
             total = total + drecv[at_col(k), j].astype(jnp.float32)
-        grad_ref[j] = jnp.where(lane_half * half + j < own_count, total, 0.0).astype(jnp.bfloat16)
+        mixed[...] = jnp.where(lane_half * half + j < own_count, total, 0.0)
+        one, two = mixed[even, :], mixed[odd, :]
+        natural[j] = jnp.where(low, one, pltpu.roll(two, TILE, 1))
+        natural[j + half] = jnp.where(low, pltpu.roll(one, TILE, 1), two)
+    for j in range(TILE // 2):
+        grad_ref[:, j * LANES : (j + 1) * LANES] = natural[:, j, :].astype(jnp.bfloat16)
 
     for c in range(chunks):
         for k in range(1, group):
@@ -313,26 +318,33 @@
     tc = tok // CHUNKS
     rows = tc // 2
     width = -(-max(slots, per_col) // LANES) * LANES
-    w = weight_tiles.reshape(2, half, TILE, TILE).transpose(1, 2, 0, 3).reshape(half, TILE, 2 * TILE)
+    w = weight_tiles.reshape(cap, TILE * TILE)
     bf16, f32, i32 = jnp.bfloat16, jnp.float32, jnp.int32
     vmem = pl.BlockSpec(memory_space=pltpu.VMEM)
     smem = pl.BlockSpec(memory_space=pltpu.SMEM)
+    hbm = pl.BlockSpec(memory_space=pltpu.HBM)
     dma = pltpu.SemaphoreType.DMA
     n_pair = ff_local // LANES
     output, grad = pl.pallas_call(
         functools.partial(kernel, n_row, n_col, per_col),
         out_shape=(
             jax.ShapeDtypeStruct((tok, ff_local), bf16),
-            jax.ShapeDtypeStruct((half, TILE, LANES), bf16),
+            jax.ShapeDtypeStruct((cap, TILE * TILE), bf16),
         ),
-        in_specs=[vmem, vmem, smem, smem, vmem],
+        in_specs=[hbm, vmem, smem, smem, hbm],
         out_specs=(vmem, vmem),
         scratch_shapes=[
             *[pltpu.VMEM((group * own_tiles, rows, LANES), bf16) for _ in range(CHUNKS)],
+            pltpu.VMEM(activations.shape, bf16),
+            pltpu.VMEM(upstream.shape, bf16),
+            pltpu.VMEM((cap, TILE // 2, LANES), f32),
+            pltpu.VMEM((TILE, LANES), f32),
+            pltpu.VMEM((half, TILE, LANES), bf16),
             pltpu.VMEM((CHUNKS, n_col, cap, rows, LANES), bf16),
             pltpu.VMEM((CHUNKS, n_col, cap, rows, LANES), bf16),
             pltpu.VMEM((n_col, half, TILE, LANES), bf16),
             pltpu.VMEM((slots, 2 * TILE, LANES), bf16),
+            pltpu.VMEM((slots, tok, LANES), bf16),
             pltpu.VMEM((8, LANES), i32),
             pltpu.VMEM((n_col, 8, LANES), i32),
             pltpu.VMEM((n_col, 8, LANES), i32),
@@ -342,8 +354,8 @@
             pltpu.SMEM((8, width), i32),
             pltpu.VMEM((slots, tc, LANES), f32),
             pltpu.VMEM((slots + 1, tc, LANES), f32),
-            pltpu.VMEM((n_pair, tc, LANES), bf16),
-            pltpu.VMEM((slots, TILE, LANES), f32),
+            pltpu.VMEM((n_pair, tok, LANES), bf16),
+            pltpu.VMEM((per_col, TILE, tok), bf16),
             pltpu.VMEM((n_col, half, TILE, LANES), bf16),
             pltpu.VMEM((n_col, half, TILE, LANES), bf16),
             dma((CHUNKS, group)), dma((CHUNKS, group)),
@@ -352,13 +364,12 @@
             dma((n_col,)), dma((n_col,)),
             dma((CHUNKS, n_col)), dma((CHUNKS, n_col)),
             dma((n_col,)), dma((n_col,)),
-            dma((2,)),
+            dma((4,)),
         ],
         compiler_params=pltpu.CompilerParams(
-            collective_id=0, has_side_effects=True, vmem_limit_bytes=48 * 1024 * 1024
+            collective_id=0, has_side_effects=True, vmem_limit_bytes=62 * 1024 * 1024
         ),
     )(activations, w, tile_ids.reshape(cap), tile_counts.reshape(1), upstream)
-    grad = grad.reshape(half, TILE, 2, TILE).transpose(2, 0, 1, 3)
     return (output, grad.reshape(1, 1, cap, TILE * TILE))
 
 

time: 46.4 us -> 44 us (0.948)
  local copies, waits for them, and re-layouts: 4.85 us -> 2.76 us
    reshape x5 -> x0, local copies, waits for them, and re-layouts: 2.43 us -> none  [the longest x3 1.46 us: body(): weight_tiles.reshape(2, half, TILE, TILE).transpose(1, 2, 0, 3)]
    unnamed x7 -> x4, local copies, waits for them, and re-layouts: 2.39 us -> 2.76 us
where the time goes in v3:
time: 44 us; the launch traced here: 43.8 us
  Pallas kernels  39.7 us (90%)
  local copies, waits for them, and re-layouts  2.76 us (6%)
  between operations  1.29 us (3%)
    pallas_call x1, Pallas kernels, body(): pl.pallas_call(functools.partial(kernel, n_row, n_col, per_col), out_shap...  39.7 us
    unnamed x4, local copies, waits for them, and re-layouts  2.76 us

profile of v3, /device:TPU:1, one launch (start us, length us, event | category | flops | bytes accessed | tf_op | source)
XLA Modules:
  0.0 43.8 jit_solution(10764166633775508896)
XLA Ops:
  1.3 39.7 %shard_map.68 = (bf16[128,3072]{1,0:T(8,128)(2,1)}, bf16[12,4096]{1,0:T(8,128)(2,1)}) custom-call(bf16[128,1536]{1,0:T(8,128)(2,1)} %x_hbm.1, bf16[12,4096]{1,0:T(8,128)(2,1)} %bitcast.5, s32[12]{0:T(128)} %bitcast.7, s32[1]{0:T(128)} %bitcast.4.cnt_ref, bf16[128,3072]{1,0:T(8,128)(2,1)} %up_hbm.1), custom_call_target="tpu_custom_call" | custom-call | tf_op jit(solution)/shard_map/pallas_call | solution.py:328
  41.0 0.0 copy-start
  41.0 2.1 %copy.10 = bf16[128,3072]{1,0:T(8,128)(2,1)} copy(bf16[128,3072]{1,0:T(8,128)(2,1)} %get-tuple-element.8) | data formatting | bytes 1572864
  43.1 0.0 copy-done
  43.1 0.7 %copy.11 = bf16[1,1,12,4096]{3,2,1,0:T(8,128)(2,1)} copy(bf16[1,1,12,4096]{3,2,1,0:T(8,128)(2,1)S(1)} %bitcast.6) | data formatting | bytes 196608
Async XLA Ops:
  41.0 2.1 %copy-start = (bf16[12,4096]{1,0:T(8,128)(2,1)S(1)}, bf16[12,4096]{1,0:T(8,128)(2,1)}, u32[]{:S(2)}) copy-start(bf16[12,4096]{1,0:T(8,128)(2,1)} %get-tuple-element.5) | copy-start | bytes 294916

commit v4 on v3

--- a/solution.py
+++ b/solution.py
@@ -67,9 +67,14 @@
         pl.semaphore_signal(barrier, inc=1, device_id={"col": at_col(k)}, device_id_type=MESH)
 
     lane8 = lax.broadcasted_iota(jnp.int32, (8, LANES), 1)
-    packed = jnp.where(lane8 == cap, cnt_ref[0], 0)
+    row8 = lax.broadcasted_iota(jnp.int32, (8, LANES), 0)
+    ids = jnp.zeros((8, LANES), jnp.int32)
     for s in range(cap):
-        packed = jnp.where(lane8 == s, ids_ref[s], packed)
+        ids = jnp.where(lane8 == s, ids_ref[s], ids)
+    feature = ids // per_col
+    hidden_tile = ids - feature * per_col
+    packed = jnp.where(row8 == 0, feature, jnp.where(row8 == 1, hidden_tile, lax.rem(hidden_tile, 2)))
+    packed = jnp.where(lane8 == cap, cnt_ref[0], packed)
     idsrc[...] = packed
     idc[col] = packed
 
@@ -158,10 +163,10 @@
         for k in range(line - 1, 0, -1):
             to = at_line(k)
             for s in range(cap):
-                sendx[c, to, s] = xg[c][sidq[to, 0, s] // per_col]
+                sendx[c, to, s] = xg[c][sidq[to, 0, s]]
             x_line(c, k, z).start()
         for s in range(cap):
-            recvx[c, z, s] = xg[c][sidq[z, 0, s] // per_col]
+            recvx[c, z, s] = xg[c][sidq[z, 0, s]]
 
     width = table.shape[1]
     lanes_s = lax.broadcasted_iota(jnp.int32, (slots, width), 1)
@@ -171,7 +176,7 @@
     lane1 = lax.broadcasted_iota(jnp.int32, (1, width), 1)
     for s in range(slots):
         b, j = s // cap, s % cap
-        f = jnp.where(j < sidc[b, 0, cap], lax.rem(sidc[b, 0, j], per_col), per_col)
+        f = jnp.where(j < sidc[b, 0, cap], sidc[b, 1, j], per_col)
         key_row = jnp.where(lane1 == s, f * slots + s, key_row)
         key_col = jnp.where(rows_s == s, f, key_col)
     ahead = jnp.where(key_row < key_col * slots + rows_s, 1, 0)
@@ -192,10 +197,10 @@
 
     def place_weights(b, carry):
         for s in range(cap):
-            f = lax.rem(sidc[b, 0, s], per_col)
+            side = sidc[b, 2, s]
             both = jnp.where(lane_half == s // half, wbuf[b, s % half].astype(jnp.float32), 0.0)
             both = both + pltpu.roll(both, TILE, 1)
-            placed = jnp.where(lane_half == lax.rem(f, 2), both, 0.0).astype(jnp.bfloat16)
+            placed = jnp.where(lane_half == side, both, 0.0).astype(jnp.bfloat16)
             wpl[b * cap + s, :TILE] = placed
             wpl[b * cap + s, TILE:] = placed
         return carry
@@ -256,8 +261,7 @@
         for j in range(half):
             parts = []
             for i in (j, j + half):
-                f = lax.rem(sidc[b, 0, i], per_col)
-                parts.append(jnp.dot(gt[f], xall[b * cap + i], preferred_element_type=jnp.float32))
+                parts.append(jnp.dot(gt[sidc[b, 1, i]], xall[b * cap + i], preferred_element_type=jnp.float32))
             turned = jnp.concatenate(parts, axis=0).T
             dsend[b, j] = (turned[:TILE] + turned[TILE:]).astype(jnp.bfloat16)
 
@@ -367,7 +371,7 @@
             dma((4,)),
         ],
         compiler_params=pltpu.CompilerParams(
-            collective_id=0, has_side_effects=True, vmem_limit_bytes=62 * 1024 * 1024
+            collective_id=0, has_side_effects=True, vmem_limit_bytes=52 * 1024 * 1024
         ),
     )(activations, w, tile_ids.reshape(cap), tile_counts.reshape(1), upstream)
     return (output, grad.reshape(1, 1, cap, TILE * TILE))

time: 44 us -> 44.1 us (level)
  local copies, waits for them, and re-layouts: 2.76 us -> 4.08 us
  Pallas kernels: 39.7 us -> 38.5 us
    unnamed x4 -> x8, local copies, waits for them, and re-layouts: 2.76 us -> 4.08 us
    pallas_call x1, Pallas kernels: 39.7 us -> 38.5 us  [body(): pl.pallas_call(functools.partial(kernel, n_row, n_col, per_col), out_shap...]
where the time goes in v4:
time: 44.1 us; the launch traced here: 43.9 us
  Pallas kernels  38.5 us (87%)
  local copies, waits for them, and re-layouts  4.08 us (9%)
  between operations  1.3 us (3%)
    pallas_call x1, Pallas kernels, body(): pl.pallas_call(functools.partial(kernel, n_row, n_col, per_col), out_shap...  38.5 us
    unnamed x8, local copies, waits for them, and re-layouts  4.08 us

profile of v4, /device:TPU:1, one launch (start us, length us, event | category | flops | bytes accessed | tf_op | source)
XLA Modules:
  0.0 43.9 jit_solution(4119906213432818332)
XLA Ops:
  1.3 0.0 copy-start.2
  1.3 0.6 %copy-done.2 = s32[1,1,12]{2,1,0:T(1,128)S(1)} copy-done((s32[1,1,12]{2,1,0:T(1,128)S(1)}, s32[1,1,12]{2,1,0:T(1,128)}, u32[]{:S(2)}) %copy-start.2) | copy-done | bytes 72
  1.9 0.0 copy-start
  1.9 1.0 %copy-done = bf16[128,1536]{1,0:T(8,128)(2,1)S(1)} copy-done((bf16[128,1536]{1,0:T(8,128)(2,1)S(1)}, bf16[128,1536]{1,0:T(8,128)(2,1)}, u32[]{:S(2)}) %copy-start) | copy-done | bytes 393240
  2.9 0.0 copy-start.1
  2.9 0.9 %copy-done.1 = bf16[1,1,12,4096]{3,2,1,0:T(8,128)(2,1)S(1)} copy-done((bf16[1,1,12,4096]{3,2,1,0:T(8,128)(2,1)S(1)}, bf16[1,1,12,4096]{3,2,1,0:T(8,128)(2,1)}, u32[]{:S(2)}) %copy-start.1) | copy-done | bytes 98328
  3.8 38.5 %shard_map.68 = (bf16[128,3072]{1,0:T(8,128)(2,1)S(1)}, bf16[12,4096]{1,0:T(8,128)(2,1)S(1)}) custom-call(bf16[128,1536]{1,0:T(8,128)(2,1)S(1)} %copy-done, bf16[12,4096]{1,0:T(8,128)(2,1)S(1)} %bitcast.5, s32[12]{0:T(128)S(1)} %bitcast.7, s32[1]{0:T(128)} %bitcast.4.cnt_ref, bf16[128,3072]{1,0:T(8,128)(2,1)} %up_hbm.1), custom_call_target="tpu_custom_call" | custom-call | tf_op jit(solution)/shard_map/pallas_call | solution.py:332
  42.3 0.9 %copy.10 = bf16[128,3072]{1,0:T(8,128)(2,1)} copy(bf16[128,3072]{1,0:T(8,128)(2,1)S(1)} %get-tuple-element.8) | data formatting | bytes 1572864
  43.2 0.7 %copy.11 = bf16[1,1,12,4096]{3,2,1,0:T(8,128)(2,1)} copy(bf16[1,1,12,4096]{3,2,1,0:T(8,128)(2,1)S(1)} %bitcast.6) | data formatting | bytes 196608
Async XLA Ops:
  1.3 0.7 %copy-start.2 = (s32[1,1,12]{2,1,0:T(1,128)S(1)}, s32[1,1,12]{2,1,0:T(1,128)}, u32[]{:S(2)}) copy-start(s32[1,1,12]{2,1,0:T(1,128)} %param.7) | copy-start | bytes 148
  1.9 1.0 %copy-start = (bf16[128,1536]{1,0:T(8,128)(2,1)S(1)}, bf16[128,1536]{1,0:T(8,128)(2,1)}, u32[]{:S(2)}) copy-start(bf16[128,1536]{1,0:T(8,128)(2,1)} %x_hbm.1) | copy-start | bytes 1179652
  2.9 0.9 %copy-start.1 = (bf16[1,1,12,4096]{3,2,1,0:T(8,128)(2,1)S(1)}, bf16[1,1,12,4096]{3,2,1,0:T(8,128)(2,1)}, u32[]{:S(2)}) copy-start(bf16[1,1,12,4096]{3,2,1,0:T(8,128)(2,1)} %param.6) | copy-start | bytes 294916

commit v5 on v4

--- a/solution.py
+++ b/solution.py
@@ -22,11 +22,11 @@
 
 def kernel(
     n_row, n_col, per_col,
-    x_hbm, w_ref, ids_ref, cnt_ref, up_hbm, out_ref, grad_ref, *scratch,
+    x_hbm, w_hbm, ids_ref, cnt_ref, up_hbm, out_ref, grad_ref, *scratch,
 ):
     xg, scratch = scratch[:CHUNKS], scratch[CHUNKS:]
     (
-        x_ref, up_ref, natural, mixed, wsrc, sendx, recvx, wbuf, wpl, xall, idsrc, idq, idc, sidq, sidc, table, stable,
+        x_ref, up_ref, w_ref, natural, mixed, wsrc, sendx, recvx, wbuf, wpl, xall, idsrc, idq, idc, sidq, sidc, table, stable,
         prod, run, g, gt, dsend, drecv,
         xg_s, xg_r, ic_s, ic_r, iq_s, iq_r, w_s, w_r, xz_s, xz_r, d_s, d_r, loc,
     ) = scratch
@@ -57,6 +57,8 @@
     copy_x = pltpu.make_async_copy(x_hbm, x_ref, loc.at[2])
     copy_up = pltpu.make_async_copy(up_hbm, up_ref, loc.at[3])
     copy_x.start()
+    copy_w = pltpu.make_async_copy(w_hbm, w_ref, loc.at[4])
+    copy_w.start()
     copy_up.start()
     barrier = pltpu.get_barrier_semaphore()
     for k in range(1, group):
@@ -123,11 +125,14 @@
         ids_col(k, col).start()
     for k in range(1, group):
         x_group(0, k, x).start()
-    for c in range(1, chunks):
+
+    def swap(c):
         pack(c)
         for k in range(1, group):
             x_group(c, k, x).start()
 
+    if chunks > 1:
+        swap(1)
     for k in range(1, n_col):
         ids_col(k, at_col(k)).wait_recv()
     for k in range(1, line):
@@ -136,20 +141,8 @@
     copy_c = pltpu.make_async_copy(idc, sidc, loc.at[1])
     copy_c.start()
 
-    lane_half = lax.broadcasted_iota(jnp.int32, (TILE, LANES), 1) // TILE
-    low = lax.broadcasted_iota(jnp.int32, (TILE // 2, LANES), 1) < TILE
-    even, odd = pl.ds(0, TILE // 2, stride=2), pl.ds(1, TILE // 2, stride=2)
-    for j in range(TILE // 2):
-        natural[:, j, :] = w_ref[:, j * LANES : (j + 1) * LANES].astype(jnp.float32)
-    for j in range(half):
-        one, two = natural[j], natural[j + half]
-        mixed[even, :] = jnp.where(low, one, pltpu.roll(two, TILE, 1))
-        mixed[odd, :] = jnp.where(low, pltpu.roll(one, TILE, 1), two)
-        wsrc[j] = mixed[...].astype(jnp.bfloat16)
-    wbuf[col] = wsrc[...]
-    for k in range(1, n_col):
-        w_col(k, col).start()
-
+    for c in range(2, chunks):
+        swap(c)
     for k in range(1, line):
         ids_line(k, at_line(k)).wait_recv()
     copy_q = pltpu.make_async_copy(idq, sidq, loc.at[0])
@@ -157,7 +150,7 @@
     copy_c.wait()
     copy_q.wait()
 
-    for c in range(chunks):
+    def send_chunk(c):
         for k in range(1, group):
             x_group(c, k, member(k)).wait_recv()
         for k in range(line - 1, 0, -1):
@@ -167,6 +160,26 @@
             x_line(c, k, z).start()
         for s in range(cap):
             recvx[c, z, s] = xg[c][sidq[z, 0, s]]
+
+    send_chunk(0)
+
+    lane_half = lax.broadcasted_iota(jnp.int32, (TILE, LANES), 1) // TILE
+    low = lax.broadcasted_iota(jnp.int32, (TILE // 2, LANES), 1) < TILE
+    even, odd = pl.ds(0, TILE // 2, stride=2), pl.ds(1, TILE // 2, stride=2)
+    copy_w.wait()
+    for j in range(TILE // 2):
+        natural[:, j, :] = w_ref[:, j * LANES : (j + 1) * LANES].astype(jnp.float32)
+    for j in range(half):
+        one, two = natural[j], natural[j + half]
+        mixed[even, :] = jnp.where(low, one, pltpu.roll(two, TILE, 1))
+        mixed[odd, :] = jnp.where(low, pltpu.roll(one, TILE, 1), two)
+        wsrc[j] = mixed[...].astype(jnp.bfloat16)
+    wbuf[col] = wsrc[...]
+    for k in range(1, n_col):
+        w_col(k, col).start()
+
+    for c in range(1, chunks):
+        send_chunk(c)
 
     width = table.shape[1]
     lanes_s = lax.broadcasted_iota(jnp.int32, (slots, width), 1)
@@ -274,8 +287,12 @@
     lax.fori_loop(0, chunks - 1, early, 0)
     hidden(chunks - 1, True)
 
+    odd_core = lax.rem(col, 2)
+    mate = 1 + odd_core * (n_col - 2)
+
     def send_terms(i, carry):
-        k = 1 + lax.rem(n_col // 2 - 1 + i, n_col - 1)
+        k = 2 - odd_core + i
+        k = k + (i + 1) // (n_col - 1) * (mate - k)
         terms(at_col(k))
         d_col(k, col).start()
         return carry
@@ -328,6 +345,7 @@
     smem = pl.BlockSpec(memory_space=pltpu.SMEM)
     hbm = pl.BlockSpec(memory_space=pltpu.HBM)
     dma = pltpu.SemaphoreType.DMA
+    in_hbm = functools.partial(pltpu.with_memory_space_constraint, memory_space=pltpu.HBM)
     n_pair = ff_local // LANES
     output, grad = pl.pallas_call(
         functools.partial(kernel, n_row, n_col, per_col),
@@ -335,12 +353,13 @@
             jax.ShapeDtypeStruct((tok, ff_local), bf16),
             jax.ShapeDtypeStruct((cap, TILE * TILE), bf16),
         ),
-        in_specs=[hbm, vmem, smem, smem, hbm],
+        in_specs=[hbm, hbm, smem, smem, hbm],
         out_specs=(vmem, vmem),
         scratch_shapes=[
             *[pltpu.VMEM((group * own_tiles, rows, LANES), bf16) for _ in range(CHUNKS)],
             pltpu.VMEM(activations.shape, bf16),
             pltpu.VMEM(upstream.shape, bf16),
+            pltpu.VMEM(w.shape, bf16),
             pltpu.VMEM((cap, TILE // 2, LANES), f32),
             pltpu.VMEM((TILE, LANES), f32),
             pltpu.VMEM((half, TILE, LANES), bf16),
@@ -368,12 +387,12 @@
             dma((n_col,)), dma((n_col,)),
             dma((CHUNKS, n_col)), dma((CHUNKS, n_col)),
             dma((n_col,)), dma((n_col,)),
-            dma((4,)),
+            dma((5,)),
         ],
         compiler_params=pltpu.CompilerParams(
-            collective_id=0, has_side_effects=True, vmem_limit_bytes=52 * 1024 * 1024
+            collective_id=0, has_side_effects=True, vmem_limit_bytes=48 * 1024 * 1024
         ),
-    )(activations, w, tile_ids.reshape(cap), tile_counts.reshape(1), upstream)
+    )(in_hbm(activations), in_hbm(w), tile_ids.reshape(cap), tile_counts.reshape(1), in_hbm(upstream))
     return (output, grad.reshape(1, 1, cap, TILE * TILE))
 
 

time: 44.1 us -> 42 us (0.952)
  local copies, waits for them, and re-layouts: 4.08 us -> 2.19 us
    unnamed x8 -> x4, local copies, waits for them, and re-layouts: 4.08 us -> 2.19 us
where the time goes in v5:
time: 42 us; the launch traced here: 41.8 us
  Pallas kernels  38.3 us (91%)
  local copies, waits for them, and re-layouts  2.19 us (5%)
  between operations  1.29 us (3%)
    pallas_call x1, Pallas kernels, body(): pl.pallas_call(functools.partial(kernel, n_row, n_col, per_col), out_shap...  38.3 us
    unnamed x4, local copies, waits for them, and re-layouts  2.19 us

profile of v5, /device:TPU:1, one launch (start us, length us, event | category | flops | bytes accessed | tf_op | source)
XLA Modules:
  0.0 41.8 jit_solution(14127482018321410508)
XLA Ops:
  1.3 0.0 copy-start
  1.3 0.6 %copy-done = s32[1,1,12]{2,1,0:T(1,128)S(1)} copy-done((s32[1,1,12]{2,1,0:T(1,128)S(1)}, s32[1,1,12]{2,1,0:T(1,128)}, u32[]{:S(2)}) %copy-start) | copy-done | bytes 72
  1.9 38.3 %shard_map.68 = (bf16[128,3072]{1,0:T(8,128)(2,1)S(1)}, bf16[12,4096]{1,0:T(8,128)(2,1)S(1)}) custom-call(bf16[128,1536]{1,0:T(8,128)(2,1)} %x_hbm.1, bf16[12,4096]{1,0:T(8,128)(2,1)} %bitcast.7, s32[12]{0:T(128)S(1)} %bitcast.6, s32[1]{0:T(128)} %bitcast.4.cnt_ref, bf16[128,3072]{1,0:T(8,128)(2,1)} %up_hbm.1), custom_call_target="tpu_custom_call" | custom-call | tf_op jit(solution)/shard_map/pallas_call | solution.py:350
  40.3 0.9 %copy.10 = bf16[128,3072]{1,0:T(8,128)(2,1)} copy(bf16[128,3072]{1,0:T(8,128)(2,1)S(1)} %get-tuple-element.8) | data formatting | bytes 1572864
  41.1 0.7 %copy.11 = bf16[1,1,12,4096]{3,2,1,0:T(8,128)(2,1)} copy(bf16[1,1,12,4096]{3,2,1,0:T(8,128)(2,1)S(1)} %bitcast.5) | data formatting | bytes 196608
Async XLA Ops:
  1.3 0.7 %copy-start = (s32[1,1,12]{2,1,0:T(1,128)S(1)}, s32[1,1,12]{2,1,0:T(1,128)}, u32[]{:S(2)}) copy-start(s32[1,1,12]{2,1,0:T(1,128)} %param.7) | copy-start | bytes 148

commit v6 on v5

--- a/solution.py
+++ b/solution.py
@@ -10,7 +10,7 @@
 TILE = 64
 LANES = 128
 CHUNKS = 4
-UNROLL = 3
+UNROLL = 4
 MESH = pl.DeviceIdType.MESH
 
 
@@ -22,15 +22,15 @@
 
 def kernel(
     n_row, n_col, per_col,
-    x_hbm, w_hbm, ids_ref, cnt_ref, up_hbm, out_ref, grad_ref, *scratch,
+    x_hbm, w_hbm, ids_hbm, cnt_ref, up_hbm, out_ref, grad_ref, *scratch,
 ):
     xg, scratch = scratch[:CHUNKS], scratch[CHUNKS:]
     (
-        x_ref, up_ref, w_ref, natural, mixed, wsrc, sendx, recvx, wbuf, wpl, xall, idsrc, idq, idc, sidq, sidc, table, stable,
+        ids_ref, x_ref, up_ref, w_ref, natural, mixed, wsrc, sendx, recvx, wbuf, wpl, xall, idsrc, idq, idc, sidq, sidc, table, stable,
         prod, run, g, gt, dsend, drecv,
         xg_s, xg_r, ic_s, ic_r, iq_s, iq_r, w_s, w_r, xz_s, xz_r, d_s, d_r, loc,
     ) = scratch
-    cap = ids_ref.shape[0]
+    cap = ids_hbm.shape[0]
     half = cap // 2
     slots = n_col * cap
     group = n_row // n_col
@@ -54,9 +54,15 @@
     def at_col(k):
         return lax.rem(col + k, n_col)
 
-    copy_x = pltpu.make_async_copy(x_hbm, x_ref, loc.at[2])
+    copy_ids = pltpu.make_async_copy(ids_hbm, ids_ref, loc.at[0])
+    copy_x = [
+        pltpu.make_async_copy(x_hbm.at[pl.ds(c * tc, tc)], x_ref.at[pl.ds(c * tc, tc)], loc.at[5 + c])
+        for c in range(chunks)
+    ]
     copy_up = pltpu.make_async_copy(up_hbm, up_ref, loc.at[3])
-    copy_x.start()
+    copy_ids.start()
+    for copy in copy_x:
+        copy.start()
     copy_w = pltpu.make_async_copy(w_hbm, w_ref, loc.at[4])
     copy_w.start()
     copy_up.start()
@@ -71,6 +77,7 @@
     lane8 = lax.broadcasted_iota(jnp.int32, (8, LANES), 1)
     row8 = lax.broadcasted_iota(jnp.int32, (8, LANES), 0)
     ids = jnp.zeros((8, LANES), jnp.int32)
+    copy_ids.wait()
     for s in range(cap):
         ids = jnp.where(lane8 == s, ids_ref[s], ids)
     feature = ids // per_col
@@ -81,13 +88,13 @@
     idc[col] = packed
 
     def pack(c):
+        copy_x[c].wait()
         for t in range(own_tiles):
             lanes = slice(t * TILE, (t + 1) * TILE)
             top = x_ref[c * tc : c * tc + packed_rows, lanes].astype(jnp.float32)
             bottom = x_ref[c * tc + packed_rows : (c + 1) * tc, lanes].astype(jnp.float32)
             xg[c][x * own_tiles + t] = jnp.concatenate([top, bottom], axis=1).astype(jnp.bfloat16)
 
-    copy_x.wait()
     pack(0)
     pl.semaphore_wait(barrier, group + line + n_col - 3)
 
@@ -252,7 +259,7 @@
             run[r] = total
             return total
 
-        lax.fori_loop(0, slots, add_run, jnp.zeros((tc, LANES), jnp.float32), unroll=4)
+        lax.fori_loop(0, slots, add_run, jnp.zeros((tc, LANES), jnp.float32), unroll=8 if slots % 8 == 0 else 1)
 
         rows = chunk_rows(c)
 
@@ -268,7 +275,7 @@
                 gt[2 * p + 1] = both[TILE:]
             return carry
 
-        lax.fori_loop(0, n_pair, gelu_pair, 0, unroll=UNROLL)
+        lax.fori_loop(0, n_pair, gelu_pair, 0, unroll=UNROLL if n_pair % UNROLL == 0 else 1)
 
     def terms(b):
         for j in range(half):
@@ -353,10 +360,11 @@
             jax.ShapeDtypeStruct((tok, ff_local), bf16),
             jax.ShapeDtypeStruct((cap, TILE * TILE), bf16),
         ),
-        in_specs=[hbm, hbm, smem, smem, hbm],
+        in_specs=[hbm, hbm, hbm, smem, hbm],
         out_specs=(vmem, vmem),
         scratch_shapes=[
             *[pltpu.VMEM((group * own_tiles, rows, LANES), bf16) for _ in range(CHUNKS)],
+            pltpu.SMEM((cap,), i32),
             pltpu.VMEM(activations.shape, bf16),
             pltpu.VMEM(upstream.shape, bf16),
             pltpu.VMEM(w.shape, bf16),
@@ -387,12 +395,12 @@
             dma((n_col,)), dma((n_col,)),
             dma((CHUNKS, n_col)), dma((CHUNKS, n_col)),
             dma((n_col,)), dma((n_col,)),
-            dma((5,)),
+            dma((5 + CHUNKS,)),
         ],
         compiler_params=pltpu.CompilerParams(
             collective_id=0, has_side_effects=True, vmem_limit_bytes=48 * 1024 * 1024
         ),
-    )(in_hbm(activations), in_hbm(w), tile_ids.reshape(cap), tile_counts.reshape(1), in_hbm(upstream))
+    )(in_hbm(activations), in_hbm(w), in_hbm(tile_ids.reshape(cap)), tile_counts.reshape(1), in_hbm(upstream))
     return (output, grad.reshape(1, 1, cap, TILE * TILE))
 
 

time: 42 us -> 40.5 us (0.964)
  Pallas kernels: 38.3 us -> 37.5 us
  local copies, waits for them, and re-layouts: 2.19 us -> 1.54 us
    pallas_call x1, Pallas kernels: 38.3 us -> 37.5 us  [body(): pl.pallas_call(functools.partial(kernel, n_row, n_col, per_col), out_shap...]
    unnamed x4 -> x2, local copies, waits for them, and re-layouts: 2.19 us -> 1.54 us
where the time goes in v6:
time: 40.5 us; the launch traced here: 40.3 us
  Pallas kernels  37.5 us (93%)
  local copies, waits for them, and re-layouts  1.54 us (4%)
  between operations  1.29 us (3%)
    pallas_call x1, Pallas kernels, body(): pl.pallas_call(functools.partial(kernel, n_row, n_col, per_col), out_shap...  37.5 us
    unnamed x2, local copies, waits for them, and re-layouts  1.54 us

profile of v6, /device:TPU:1, one launch (start us, length us, event | category | flops | bytes accessed | tf_op | source)
XLA Modules:
  0.0 40.3 jit_solution(5269510278713056968)
XLA Ops:
  1.3 37.5 %shard_map.68 = (bf16[128,3072]{1,0:T(8,128)(2,1)S(1)}, bf16[12,4096]{1,0:T(8,128)(2,1)S(1)}) custom-call(bf16[128,1536]{1,0:T(8,128)(2,1)} %x_hbm.1, bf16[12,4096]{1,0:T(8,128)(2,1)} %bitcast.6, s32[12]{0:T(128)} %bitcast.7, s32[1]{0:T(128)} %bitcast.4.cnt_ref, bf16[128,3072]{1,0:T(8,128)(2,1)} %up_hbm.1), custom_call_target="tpu_custom_call" | custom-call | tf_op jit(solution)/shard_map/pallas_call | solution.py:357
  38.8 0.9 %copy.10 = bf16[128,3072]{1,0:T(8,128)(2,1)} copy(bf16[128,3072]{1,0:T(8,128)(2,1)S(1)} %get-tuple-element.8) | data formatting | bytes 1572864
  39.7 0.7 %copy.11 = bf16[1,1,12,4096]{3,2,1,0:T(8,128)(2,1)} copy(bf16[1,1,12,4096]{3,2,1,0:T(8,128)(2,1)S(1)} %bitcast.5) | data formatting | bytes 196608

commit v7 on v6

--- a/solution.py
+++ b/solution.py
@@ -10,7 +10,7 @@
 TILE = 64
 LANES = 128
 CHUNKS = 4
-UNROLL = 4
+UNROLL = 6
 MESH = pl.DeviceIdType.MESH
 
 
@@ -259,7 +259,7 @@
             run[r] = total
             return total
 
-        lax.fori_loop(0, slots, add_run, jnp.zeros((tc, LANES), jnp.float32), unroll=8 if slots % 8 == 0 else 1)
+        lax.fori_loop(0, slots, add_run, jnp.zeros((tc, LANES), jnp.float32), unroll=12 if slots % 12 == 0 else 1)
 
         rows = chunk_rows(c)
 
@@ -304,7 +304,11 @@
         d_col(k, col).start()
         return carry
 
-    lax.fori_loop(0, n_col - 1, send_terms, 0)
+    if n_col <= 4:
+        for i in range(n_col - 1):
+            send_terms(i, 0)
+    else:
+        lax.fori_loop(0, n_col - 1, send_terms, 0)
     terms(col)
     for k in range(1, n_col):
         d_col(k, at_col(k)).wait_recv()

time: 40.5 us -> 40.3 us (level)
  no operation moved by 1% of the time
where the time goes in v7:
time: 40.3 us; the launch traced here: 40.1 us
  Pallas kernels  37.3 us (93%)
  local copies, waits for them, and re-layouts  1.54 us (4%)
  between operations  1.29 us (3%)
    pallas_call x1, Pallas kernels, body(): pl.pallas_call(functools.partial(kernel, n_row, n_col, per_col), out_shap...  37.3 us
    unnamed x2, local copies, waits for them, and re-layouts  1.54 us

profile of v7, /device:TPU:1, one launch (start us, length us, event | category | flops | bytes accessed | tf_op | source)
XLA Modules:
  0.0 40.1 jit_solution(14096279430436451251)
XLA Ops:
  1.3 37.3 %shard_map.68 = (bf16[128,3072]{1,0:T(8,128)(2,1)S(1)}, bf16[12,4096]{1,0:T(8,128)(2,1)S(1)}) custom-call(bf16[128,1536]{1,0:T(8,128)(2,1)} %x_hbm.1, bf16[12,4096]{1,0:T(8,128)(2,1)} %bitcast.6, s32[12]{0:T(128)} %bitcast.7, s32[1]{0:T(128)} %bitcast.4.cnt_ref, bf16[128,3072]{1,0:T(8,128)(2,1)} %up_hbm.1), custom_call_target="tpu_custom_call" | custom-call | tf_op jit(solution)/shard_map/pallas_call | solution.py:361
  38.6 0.9 %copy.10 = bf16[128,3072]{1,0:T(8,128)(2,1)} copy(bf16[128,3072]{1,0:T(8,128)(2,1)S(1)} %get-tuple-element.8) | data formatting | bytes 1572864
  39.4 0.7 %copy.11 = bf16[1,1,12,4096]{3,2,1,0:T(8,128)(2,1)} copy(bf16[1,1,12,4096]{3,2,1,0:T(8,128)(2,1)S(1)} %bitcast.5) | data formatting | bytes 196608

commit v8 on v7

--- a/solution.py
+++ b/solution.py
@@ -95,7 +95,6 @@
             bottom = x_ref[c * tc + packed_rows : (c + 1) * tc, lanes].astype(jnp.float32)
             xg[c][x * own_tiles + t] = jnp.concatenate([top, bottom], axis=1).astype(jnp.bfloat16)
 
-    pack(0)
     pl.semaphore_wait(barrier, group + line + n_col - 3)
 
     def remote(src, dst, send, recv, target):
@@ -130,6 +129,7 @@
 
     for k in range(1, n_col):
         ids_col(k, col).start()
+    pack(0)
     for k in range(1, group):
         x_group(0, k, x).start()
 

time: 40.3 us -> 40.3 us (level)
  no operation moved by 1% of the time
where the time goes in v8:
time: 40.3 us; the launch traced here: 40.1 us
  Pallas kernels  37.3 us (93%)
  local copies, waits for them, and re-layouts  1.54 us (4%)
  between operations  1.29 us (3%)
    pallas_call x1, Pallas kernels, body(): pl.pallas_call(functools.partial(kernel, n_row, n_col, per_col), out_shap...  37.3 us
    unnamed x2, local copies, waits for them, and re-layouts  1.54 us

profile of v8, /device:TPU:1, one launch (start us, length us, event | category | flops | bytes accessed | tf_op | source)
XLA Modules:
  0.0 40.1 jit_solution(12770199624160123943)
XLA Ops:
  1.3 37.3 %shard_map.68 = (bf16[128,3072]{1,0:T(8,128)(2,1)S(1)}, bf16[12,4096]{1,0:T(8,128)(2,1)S(1)}) custom-call(bf16[128,1536]{1,0:T(8,128)(2,1)} %x_hbm.1, bf16[12,4096]{1,0:T(8,128)(2,1)} %bitcast.6, s32[12]{0:T(128)} %bitcast.7, s32[1]{0:T(128)} %bitcast.4.cnt_ref, bf16[128,3072]{1,0:T(8,128)(2,1)} %up_hbm.1), custom_call_target="tpu_custom_call" | custom-call | tf_op jit(solution)/shard_map/pallas_call | solution.py:361
  38.6 0.9 %copy.10 = bf16[128,3072]{1,0:T(8,128)(2,1)} copy(bf16[128,3072]{1,0:T(8,128)(2,1)S(1)} %get-tuple-element.8) | data formatting | bytes 1572864
  39.4 0.7 %copy.11 = bf16[1,1,12,4096]{3,2,1,0:T(8,128)(2,1)} copy(bf16[1,1,12,4096]{3,2,1,0:T(8,128)(2,1)S(1)} %bitcast.5) | data formatting | bytes 196608
